TPU v7x, 512 devices: a whole 4x8x8 slice. The times are simulated.
512 devices in a mesh: grp: 16 (over y_hi, x), seq: 32 (over y_lo, z, core).
Axes of the slice: x: 4, y: 8 (y_hi: 4, y_lo: 2; y = y_hi * 2 + y_lo), z: 8, core: 2. Of those that a mesh axis runs over, the one named last changes fastest.
Arguments:
- giant_q: bfloat16 [16, 4096, 2048], P('grp', 'seq'), may hold values from -192 to 192
- giant_k: bfloat16 [16, 4096, 2048], P('grp', 'seq'), may hold values from -6 to 6
- giant_v: bfloat16 [16, 4096, 2048], P('grp', 'seq'), may hold values from -6 to 6
- giant_len: int32 [16], replicated, may hold values from 2048 to 4096, as said below
- short_q: bfloat16 [16, 32, 128, 2048], P('grp', 'seq'), may hold values from -6 to 6
- short_k: bfloat16 [16, 32, 128, 2048], P('grp', 'seq'), may hold values from -6 to 6
- short_v: bfloat16 [16, 32, 128, 2048], P('grp', 'seq'), may hold values from -6 to 6
- short_len: int32 [16, 32], replicated, may hold values from 32 to 128, as said below
- short_move: int32 [16, 32], replicated, may hold values from 0 to 1
Outputs:
- giant_out: bfloat16 [16, 4096, 2048], P('grp', 'seq')
- short_out: bfloat16 [16, 32, 2, 128, 2048], P('grp', 'seq')
Inputs may be any that keep to these rules, and one draw needn't show every extreme that they name: `giant_len`: residues of group g's giant protein; positions at or past it are padding; some group's protein fills all 4096 positions. `short_len`: residues of the short protein at [g, s]; slots at or past it are padding; some protein fills all 128 slots.
All inputs are finite; a program needn't handle non-finite values.
Results may differ from a plain program's by a relative error of at most 0.0068.
Values may be sent and summed in bfloat16 or wider, within the bound.
A program may use at most 64 MiB of HBM per device.

v0:
```python
import math

import jax
import jax.numpy as jnp
from jax import lax
from jax.sharding import PartitionSpec as P

HD = 64
HEADS = 32


rotary_base = 10000.0


def from_behind(shard, axis, by):
    devices = lax.axis_size(axis)
    return lax.ppermute(shard, axis, [(i, (i + by) % devices) for i in range(devices)])


def rotary(values_in, places):
    half_dim = values_in.shape[-1] // 2
    frequency = rotary_base ** (
        -(jnp.arange(half_dim, dtype=jnp.float32) * 2.0) / values_in.shape[-1]
    )
    angles = places[:, None] * frequency[None, :]
    cosine = jnp.concatenate([jnp.cos(angles), jnp.cos(angles)], -1)[:, None, :]
    sine_part = jnp.concatenate([jnp.sin(angles), jnp.sin(angles)], -1)[:, None, :]
    turned = jnp.concatenate([-values_in[..., half_dim:], values_in[..., :half_dim]], -1)
    return values_in * cosine + turned * sine_part


def attend(query_rows, key_rows, value_rows, live_keys):
    scores = jnp.einsum(
        "qhd,khd->hqk", query_rows, key_rows, preferred_element_type=jnp.float32
    ) / math.sqrt(HD)
    scores = jnp.where(live_keys[None, None, :], scores, -1e30)
    running_max = jnp.max(scores, -1, keepdims=True)
    weights = jnp.where(live_keys[None, None, :], jnp.exp(scores - running_max), 0.0)
    weight_sum = jnp.sum(weights, -1)
    attended = jnp.einsum(
        "hqk,khd->qhd", weights.astype(jnp.bfloat16), value_rows, preferred_element_type=jnp.float32
    )
    return attended / jnp.transpose(weight_sum)[:, :, None]


def attend_blocked(query_rows, key_rows, value_rows, live_keys):
    row_total = query_rows.shape[0]
    block_rows = math.gcd(512, row_total)
    grouped = query_rows.reshape(
        row_total // block_rows, block_rows, query_rows.shape[1], query_rows.shape[2]
    )

    def one_block(query_block):
        return attend(query_block, key_rows, value_rows, live_keys).astype(jnp.bfloat16)

    attended = lax.map(one_block, grouped)
    return attended.reshape(row_total, query_rows.shape[1], query_rows.shape[2])


def per_device(
    giant_q, giant_k, giant_v, giant_len, short_q, short_k, short_v, short_len, short_move
):
    tok_rows = giant_q.shape[1]
    feature_width = giant_q.shape[2]
    seq_count = lax.axis_size("seq")
    seq_index = lax.axis_index("seq")
    grp_index = lax.axis_index("grp")
    protein_len = lax.dynamic_index_in_dim(giant_len, grp_index, 0, keepdims=False)
    positions = seq_index * tok_rows + jnp.arange(tok_rows, dtype=jnp.int32)
    place_float = positions.astype(jnp.float32)
    queries = rotary(
        giant_q[0].reshape(tok_rows, HEADS, HD).astype(jnp.float32), place_float
    ).astype(jnp.bfloat16)
    keys_rot = rotary(
        giant_k[0].reshape(tok_rows, HEADS, HD).astype(jnp.float32), place_float
    ).astype(jnp.bfloat16)
    values = giant_v[0].reshape(tok_rows, HEADS, HD)
    head_share = HEADS // seq_count
    live_keys = jnp.arange(tok_rows * seq_count, dtype=jnp.int32) < protein_len

    def by_heads(tensor):
        return tensor.reshape(tok_rows, seq_count, head_share, HD)

    attended = attend_blocked(
        lax.all_to_all(by_heads(queries), "seq", split_axis=1, concat_axis=0, tiled=True)[:, 0],
        lax.all_to_all(by_heads(keys_rot), "seq", split_axis=1, concat_axis=0, tiled=True)[:, 0],
        lax.all_to_all(by_heads(values), "seq", split_axis=1, concat_axis=0, tiled=True)[:, 0],
        live_keys,
    )
    joined = lax.all_to_all(attended[:, None], "seq", split_axis=0, concat_axis=1, tiled=True)
    giant_rows = joined.reshape(tok_rows, feature_width)
    giant_rows = jnp.where(
        (positions < protein_len)[:, None], giant_rows, jnp.zeros_like(giant_rows)
    )
    giant_out = giant_rows.reshape(1, tok_rows, feature_width)
    slot_count = short_q.shape[2]
    slot_float = jnp.arange(slot_count, dtype=jnp.int32).astype(jnp.float32)
    short_query = rotary(
        short_q[0, 0].reshape(slot_count, HEADS, HD).astype(jnp.float32), slot_float
    ).astype(jnp.bfloat16)
    short_key = rotary(
        short_k[0, 0].reshape(slot_count, HEADS, HD).astype(jnp.float32), slot_float
    ).astype(jnp.bfloat16)
    short_value = short_v[0, 0].reshape(slot_count, HEADS, HD)
    len_row = lax.dynamic_index_in_dim(short_len, grp_index, 0, keepdims=False)
    move_row = lax.dynamic_index_in_dim(short_move, grp_index, 0, keepdims=False)
    own_len = lax.dynamic_index_in_dim(len_row, seq_index, 0, keepdims=False)
    own_move = lax.dynamic_index_in_dim(move_row, seq_index, 0, keepdims=False)
    empty_rows = jnp.zeros((slot_count, feature_width), jnp.bfloat16)
    live_slots = jnp.arange(slot_count, dtype=jnp.int32) < own_len
    attended = attend(short_query, short_key, short_value, live_slots)
    attended = jnp.where(live_slots[:, None, None], attended, 0.0)
    result = attended.reshape(slot_count, feature_width).astype(jnp.bfloat16)
    staying = jnp.where(own_move == 0, result, empty_rows)
    leaving = jnp.where(own_move == 1, result, empty_rows)
    incoming = from_behind(leaving, "grp", 1)
    short_out = jnp.stack([staying, incoming]).reshape(1, 1, 2, slot_count, feature_width)
    return (giant_out, short_out)


def solution(mesh):
    in_specs = (
        P("grp", "seq", None),
        P("grp", "seq", None),
        P("grp", "seq", None),
        P(),
        P("grp", "seq", None, None),
        P("grp", "seq", None, None),
        P("grp", "seq", None, None),
        P(),
        P(),
    )
    out_specs = (P("grp", "seq", None), P("grp", "seq", None, None, None))
    return jax.shard_map(
        per_device, mesh=mesh, in_specs=in_specs, out_specs=out_specs, check_vma=False
    )
```

profile of v0, /device:TPU:1, one launch (start us, length us, event | category | flops | bytes accessed | tf_op | source)
XLA Modules:
  0.0 207.7 jit_solution(10755948291556074263)
XLA Ops:
  5.3 28.6 %all_to_all.60 = bf16[128,32,1,64]{0,3,2,1:T(8,128)(2,1)} all-to-all(bf16[128,32,1,64]{0,3,2,1:T(8,128)(2,1)S(1)} %get-tuple-element.87), channel_id=1, replica_groups=mesh['grp'=16,'seq'=32] {'seq'}, dimensions={1} | all-to-all | bytes 1048576 | tf_op jit(solution)/shard_map/all_to_all | solution.py:85
  33.9 5.5 %all-to-all-start.1 = ((bf16[128,32,1,64]{0,3,2,1:T(8,128)(2,1)}), bf16[128,32,1,64]{0,3,2,1:T(8,128)(2,1)S(1)}, u32[]{:S(2)}, u32[]{:S(2)}) async-start(bf16[128,32,1,64]{0,3,2,1:T(8,128)(2,1)} %get-tuple-element.86), calls=%async_computation.1 | async-start | bytes 1048576 | tf_op jit(solution)/shard_map/all_to_all | solution.py:86
  40.3 14.7 %all-to-all-done.1 = bf16[128,32,1,64]{0,3,2,1:T(8,128)(2,1)S(1)} async-done(((bf16[128,32,1,64]{0,3,2,1:T(8,128)(2,1)}), bf16[128,32,1,64]{0,3,2,1:T(8,128)(2,1)S(1)}, u32[]{:S(2)}, u32[]{:S(2)}) %all-to-all-start.1) | async-done | bytes 524320 | tf_op jit(solution)/shard_map/all_to_all | solution.py:86
  55.1 5.5 %all-to-all-start.2 = ((bf16[128,32,1,64]{0,3,2,1:T(8,128)(2,1)}), bf16[128,32,1,64]{0,3,2,1:T(8,128)(2,1)}, u32[]{:S(2)}, u32[]{:S(2)}) async-start(bf16[128,32,1,64]{0,3,2,1:T(8,128)(2,1)} %bitcast.16), calls=%async_computation.2 | async-start | bytes 1048576 | tf_op jit(solution)/shard_map/all_to_all | solution.py:87
  68.6 2.0 copy.62
  72.5 3.9 %fusion.64 = (f32[32,128]{1,0:T(8,128)S(1)}, bf16[32,128,128]{1,2,0:T(8,128)(2,1)}) fusion(pred[128]{0:T(512)(128)(4,1)S(1)} %iota_compare_fusion.1, f32[128,32,32]{0,2,1:T(8,128)} %slice.39, f32[128,32,32]{0,2,1:T(8,128)} %get-tuple-element.102, f32[128,32,32]{0,2,1:T(8,128)} %slice.37, f32[128,32,32]{0,2,1:T(8,128)} %get-tuple-element.103, ...), kind=kOutput, calls=%fused_computation.82 | convolution fusion | flops 73400448 | bytes 4276352 | tf_op jit(solution)/shard_map/sub | solution.py:38
  79.4 52.8 %while.11 = (s32[]{:T(128)}, bf16[8,512,1,64]{1,3,2,0:T(8,128)(2,1)S(1)}, bf16[8,512,1,64]{1,3,2,0:T(8,128)(2,1)S(1)}, bf16[4096,1,64]{0,2,1:T(8,128)(2,1)S(1)},...) while((s32[]{:T(128)}, bf16[8,512,1,64]{1,3,2,0:T(8,128)(2,1)S(1)}, ...), condition=%wide.region_3.4_spmd.clone, body=%wide.region_0.3_spmd.clone.sunk | while | flops 564202496 | bytes 26372192 | solution.py:56
  81.5 2.6 %fusion.83 = f32[512]{0:T(512)S(1)} fusion(f32[512,4096]{1,0:T(8,128)S(1)} %get-tuple-element.145, f32[512]{0:T(512)S(1)} %get-tuple-element.146, pred[4096]{0:T(1024)(128)(4,1)S(1)} %iota_compare_fusion.3), kind=kLoop, calls=%fused_computation.4.clone.1 | loop fusion | flops 10485248 | bytes 8396800 | tf_op jit(solution)/shard_map/while/body/eval_jaxpr/reduce_sum | solution.py:39
  84.1 1.9 fusion.84
  88.1 2.6 %fusion.83 = f32[512]{0:T(512)S(1)} fusion(f32[512,4096]{1,0:T(8,128)S(1)} %get-tuple-element.145, f32[512]{0:T(512)S(1)} %get-tuple-element.146, pred[4096]{0:T(1024)(128)(4,1)S(1)} %iota_compare_fusion.3), kind=kLoop, calls=%fused_computation.4.clone.1 | loop fusion | flops 10485248 | bytes 8396800 | tf_op jit(solution)/shard_map/while/body/eval_jaxpr/reduce_sum | solution.py:39
  90.7 1.9 fusion.84
  94.7 2.6 %fusion.83 = f32[512]{0:T(512)S(1)} fusion(f32[512,4096]{1,0:T(8,128)S(1)} %get-tuple-element.145, f32[512]{0:T(512)S(1)} %get-tuple-element.146, pred[4096]{0:T(1024)(128)(4,1)S(1)} %iota_compare_fusion.3), kind=kLoop, calls=%fused_computation.4.clone.1 | loop fusion | flops 10485248 | bytes 8396800 | tf_op jit(solution)/shard_map/while/body/eval_jaxpr/reduce_sum | solution.py:39
  101.3 2.6 %fusion.83 = f32[512]{0:T(512)S(1)} fusion(f32[512,4096]{1,0:T(8,128)S(1)} %get-tuple-element.145, f32[512]{0:T(512)S(1)} %get-tuple-element.146, pred[4096]{0:T(1024)(128)(4,1)S(1)} %iota_compare_fusion.3), kind=kLoop, calls=%fused_computation.4.clone.1 | loop fusion | flops 10485248 | bytes 8396800 | tf_op jit(solution)/shard_map/while/body/eval_jaxpr/reduce_sum | solution.py:39
  103.9 1.9 fusion.84
  107.9 2.6 %fusion.83 = f32[512]{0:T(512)S(1)} fusion(f32[512,4096]{1,0:T(8,128)S(1)} %get-tuple-element.145, f32[512]{0:T(512)S(1)} %get-tuple-element.146, pred[4096]{0:T(1024)(128)(4,1)S(1)} %iota_compare_fusion.3), kind=kLoop, calls=%fused_computation.4.clone.1 | loop fusion | flops 10485248 | bytes 8396800 | tf_op jit(solution)/shard_map/while/body/eval_jaxpr/reduce_sum | solution.py:39
  114.5 2.6 %fusion.83 = f32[512]{0:T(512)S(1)} fusion(f32[512,4096]{1,0:T(8,128)S(1)} %get-tuple-element.145, f32[512]{0:T(512)S(1)} %get-tuple-element.146, pred[4096]{0:T(1024)(128)(4,1)S(1)} %iota_compare_fusion.3), kind=kLoop, calls=%fused_computation.4.clone.1 | loop fusion | flops 10485248 | bytes 8396800 | tf_op jit(solution)/shard_map/while/body/eval_jaxpr/reduce_sum | solution.py:39
  121.1 2.6 %fusion.83 = f32[512]{0:T(512)S(1)} fusion(f32[512,4096]{1,0:T(8,128)S(1)} %get-tuple-element.145, f32[512]{0:T(512)S(1)} %get-tuple-element.146, pred[4096]{0:T(1024)(128)(4,1)S(1)} %iota_compare_fusion.3), kind=kLoop, calls=%fused_computation.4.clone.1 | loop fusion | flops 10485248 | bytes 8396800 | tf_op jit(solution)/shard_map/while/body/eval_jaxpr/reduce_sum | solution.py:39
  123.7 1.9 fusion.84
  127.7 2.6 %fusion.83 = f32[512]{0:T(512)S(1)} fusion(f32[512,4096]{1,0:T(8,128)S(1)} %get-tuple-element.145, f32[512]{0:T(512)S(1)} %get-tuple-element.146, pred[4096]{0:T(1024)(128)(4,1)S(1)} %iota_compare_fusion.3), kind=kLoop, calls=%fused_computation.4.clone.1 | loop fusion | flops 10485248 | bytes 8396800 | tf_op jit(solution)/shard_map/while/body/eval_jaxpr/reduce_sum | solution.py:39
  135.5 22.6 %reduce.4 = bf16[4096,64]{1,0:T(8,128)(2,1)S(1)} reduce(bf16[4096,1,1,64]{3,2,1,0:T(2,128)(2,1)S(1)} %reshape.261, bf16[]{:T(256)} %broadcast.168), dimensions={1,2}, to_apply=%reshape.261.reduce_sub_computation | reduce | bytes 1048578 | tf_op jit(solution)/shard_map/broadcast_in_dim;reshape | solution.py:90
  159.7 8.3 %all-to-all-start.3 = ((bf16[32,2,4096]{2,1,0:T(2,128)(2,1)}), bf16[32,2,4096]{2,1,0:T(2,128)(2,1)S(1)}, u32[]{:S(2)}, u32[]{:S(2)}) async-start(bf16[32,2,4096]{2,1,0:T(2,128)(2,1)} %reshape.262), calls=%async_computation.3 | async-start | bytes 1048576 | tf_op jit(solution)/shard_map/all_to_all | solution.py:90
  170.0 3.1 %collective-permute-start = (bf16[128,2048]{1,0:T(8,128)(2,1)S(1)}, bf16[128,2048]{1,0:T(8,128)(2,1)S(1)}, u32[]{:S(2)}, u32[]{:S(2)}) collective-permute-start(bf16[128,2048]{1,0:T(8,128)(2,1)S(1)} %copy.64), channel_id=1, source_target_pairs={{0,32},{32,64},{64,96},{96,128},{128,160},{160,192},{192,224},{224... | collective-permute-start | bytes 1572872 | tf_op jit(solution)/shard_map/ppermute | solution.py:17
  174.1 27.7 %collective-permute-done = bf16[128,2048]{1,0:T(8,128)(2,1)S(1)} collective-permute-done((bf16[128,2048]{1,0:T(8,128)(2,1)S(1)}, bf16[128,2048]{1,0:T(8,128)(2,1)S(1)}, u32[]{:S(2)}, u32[]{:S(2)}) %collective-permute-start) | collective-permute-done | bytes 524320 | tf_op jit(solution)/shard_map/ppermute | solution.py:17
  204.0 2.3 %copy.58 = bf16[4096,1,1,64]{0,3,2,1:T(8,128)(2,1)S(1)} copy(bf16[4096,1,1,64]{3,2,1,0:T(2,128)(2,1)S(1)} %reshape.263) | data formatting | bytes 1048576 | tf_op jit(solution)/shard_map/all_to_all | solution.py:90
  (84 shorter events, 52.9 us)
Async XLA Ops:
  0.7 38.7 %copy-start.5 = (bf16[1,128,2048]{2,1,0:T(8,128)(2,1)S(1)}, bf16[1,128,2048]{2,1,0:T(8,128)(2,1)}, u32[]{:S(2)}) copy-start(bf16[1,128,2048]{2,1,0:T(8,128)(2,1)} %param.13) | copy-start | bytes 1572868
  3.5 59.4 %copy-start.6 = (bf16[1,1,128,2048]{3,2,1,0:T(8,128)(2,1)S(1)}, bf16[1,1,128,2048]{3,2,1,0:T(8,128)(2,1)}, u32[]{:S(2)}) copy-start(bf16[1,1,128,2048]{3,2,1,0:T(8,128)(2,1)} %param.15) | copy-start | bytes 1572868
  4.0 60.1 %copy-start.7 = (s32[16]{0:T(128)S(1)}, s32[16]{0:T(128)}, u32[]{:S(2)}) copy-start(s32[16]{0:T(128)} %param.14) | copy-start | bytes 196
  33.9 21.2 %all-to-all-start.1 = ((bf16[128,32,1,64]{0,3,2,1:T(8,128)(2,1)}), bf16[128,32,1,64]{0,3,2,1:T(8,128)(2,1)S(1)}, u32[]{:S(2)}, u32[]{:S(2)}) async-start(bf16[128,32,1,64]{0,3,2,1:T(8,128)(2,1)} %get-tuple-element.86), calls=%async_computation.1 | async-start | bytes 1048576 | tf_op jit(solution)/shard_map/all_to_all | solution.py:86
  55.1 5.5 %copy-start = (bf16[128,32,1,64]{0,3,2,1:T(8,128)(2,1)}, bf16[128,32,1,64]{0,3,2,1:T(8,128)(2,1)S(1)}, u32[]{:S(2)}) copy-start(bf16[128,32,1,64]{0,3,2,1:T(8,128)(2,1)S(1)} %all-to-all-done.1) | copy-start | bytes 1572868
  55.1 22.7 %all-to-all-start.2 = ((bf16[128,32,1,64]{0,3,2,1:T(8,128)(2,1)}), bf16[128,32,1,64]{0,3,2,1:T(8,128)(2,1)}, u32[]{:S(2)}, u32[]{:S(2)}) async-start(bf16[128,32,1,64]{0,3,2,1:T(8,128)(2,1)} %bitcast.16), calls=%async_computation.2 | async-start | bytes 1048576 | tf_op jit(solution)/shard_map/all_to_all | solution.py:87
  72.5 3.9 %copy-start.2 = (bf16[128,32,1,64]{0,3,2,1:T(8,128)(2,1)S(1)}, bf16[128,32,1,64]{0,3,2,1:T(8,128)(2,1)}, u32[]{:S(2)}) copy-start(bf16[128,32,1,64]{0,3,2,1:T(8,128)(2,1)} %all_to_all.60) | copy-start | bytes 1572868
  72.5 4.7 %copy-start.1 = (bf16[128,32,1,64]{0,3,2,1:T(8,128)(2,1)S(1)}, bf16[128,32,1,64]{0,3,2,1:T(8,128)(2,1)}, u32[]{:S(2)}) copy-start(bf16[128,32,1,64]{0,3,2,1:T(8,128)(2,1)} %copy-done) | copy-start | bytes 1572868
  72.5 6.9 %copy-start.3 = (bf16[8,512,1,64]{1,3,2,0:T(8,128)(2,1)S(1)}, bf16[8,512,1,64]{1,3,2,0:T(8,128)(2,1)}, u32[]{:S(2)}) copy-start(bf16[8,512,1,64]{1,3,2,0:T(8,128)(2,1)} %custom-call) | copy-start | bytes 1572868
  132.2 0.8 copy-start.4
  159.7 43.1 %all-to-all-start.3 = ((bf16[32,2,4096]{2,1,0:T(2,128)(2,1)}), bf16[32,2,4096]{2,1,0:T(2,128)(2,1)S(1)}, u32[]{:S(2)}, u32[]{:S(2)}) async-start(bf16[32,2,4096]{2,1,0:T(2,128)(2,1)} %reshape.262), calls=%async_computation.3 | async-start | bytes 1048576 | tf_op jit(solution)/shard_map/all_to_all | solution.py:90
  170.0 31.7 %collective-permute-start = (bf16[128,2048]{1,0:T(8,128)(2,1)S(1)}, bf16[128,2048]{1,0:T(8,128)(2,1)S(1)}, u32[]{:S(2)}, u32[]{:S(2)}) collective-permute-start(bf16[128,2048]{1,0:T(8,128)(2,1)S(1)} %copy.64), channel_id=1, source_target_pairs={{0,32},{32,64},{64,96},{96,128},{128,160},{160,192},{192,224},{224... | collective-permute-start | bytes 1572872 | tf_op jit(solution)/shard_map/ppermute | solution.py:17
where the time goes:
time: 209 us; the launch traced here: 208 us
  other arithmetic  54.2 us (26%)
  waiting for transfers between devices  42.4 us (20%)
  matrix products  32.3 us (15%)
  blocking collectives  28.6 us (14%)
  local copies, waits for them, and re-layouts  25.3 us (12%)
  starting transfers between devices  22.4 us (11%)
  between operations  2.31 us (1%)
    all_to_all x1, blocking collectives, per_device(): lax.all_to_all(by_heads(queries), 'seq', split_axis=1, concat_axis=0, til...  28.6 us
    ppermute x1, waiting for transfers between devices, from_behind(): lax.ppermute(shard, axis, [(i, (i + by) % devices) for i in range(devices)])  27.7 us
    another operation x1, other arithmetic, per_device(): attended[:, None]  22.6 us
    reduce_sum x8, other arithmetic, attend(): weight_sum = jnp.sum(weights, -1)  20.5 us
    dot_general x9, matrix products, attend(): jnp.einsum('hqk,khd->qhd', weights.astype(jnp.bfloat16), value_rows, pref...  17 us
    all_to_all x1, waiting for transfers between devices, per_device(): lax.all_to_all(by_heads(keys_rot), 'seq', split_axis=1, concat_axis=0, ti...  14.7 us
    unnamed x27, local copies, waits for them, and re-layouts  12.1 us
    dot_general x8, matrix products, attend(): jnp.einsum('qhd,khd->hqk', query_rows, key_rows, preferred_element_type=j...  11.4 us
  transfers between devices with their start and end apart: 4, of which 2 were waited for; matrix products, arithmetic and copies ran while one was open for 10% of the time, Pallas kernels for 0%

commit v1 on v0

v1 whole, which is shorter than its diff:
```python
import functools
import math

import jax
import jax.numpy as jnp
import numpy as np
from jax import lax
from jax.experimental import pallas as pl
from jax.experimental.pallas import tpu as pltpu
from jax.sharding import PartitionSpec as P

HD = 64
HEADS = 32
TOK = 128
FEAT = HEADS * HD
LANES = 128
PAIRS = FEAT // LANES
NY, NZ, NC = 2, 8, 2
SEQ = NY * NZ * NC
NTOK = SEQ * TOK
PER = NY * NC
CHUNK = PER * TOK
HALF = NTOK // 2
LOW = -1e30
MESH = pl.DeviceIdType.MESH
f32 = jnp.float32
bf16 = jnp.bfloat16


def angle_table():
    half = HD // 2
    frequency = np.power(10000.0, -(np.arange(half, dtype=np.float64) * 2.0) / HD)
    places = np.arange(NTOK, dtype=np.float32)
    angles = (places[:, None] * frequency.astype(np.float32)[None, :]).astype(np.float64)
    cosine, sine = np.cos(angles), np.sin(angles)
    return np.concatenate([cosine, cosine, -sine, sine], -1).astype(np.float32)


def offset(step):
    return ((step + 1) // 2) * (2 * (step % 2) - 1)


def lanes(rows):
    return lax.broadcasted_iota(jnp.int32, (rows, LANES), 1)


def turn_matrix():
    row = lax.broadcasted_iota(jnp.int32, (LANES, LANES), 0)
    col = lax.broadcasted_iota(jnp.int32, (LANES, LANES), 1)
    partner = jnp.where(col % HD < HD // 2, col + HD // 2, col - HD // 2)
    return jnp.where(row == partner, 1.0, 0.0).astype(bf16)


def swap(x):
    return pltpu.roll(x, HD, 1)


def main_kernel(
    glen, slen, smove, table, gq, gk, gv, sq, sk, sv,
    o_recv, stay_out, in_out,
    xin, tab, cosine, sine, qpack, kvpack, qin, kvin, qaug, acc, top, opack, stay, leave,
    in_sem, tab_sem, own_sem, q_ss, q_rs, kv_ss, kv_rs, o_ss, o_rs, move_sem,
):
    me = lax.axis_index("seq")
    grp = lax.axis_index("grp")
    groups = lax.axis_size("grp")
    core, zed, why = me % NC, (me // NC) % NZ, me // (NC * NZ)
    mine = why * NC + core

    def seq_at(i, z):
        return ((i // NC) * NZ + (z + NZ) % NZ) * NC + i % NC

    def target(step, i):
        return seq_at(i, zed - offset(step))

    def source(step, i):
        return seq_at(i, zed + offset(step))

    def dev(seq):
        return {"grp": grp, "seq": seq}

    def other(t):
        return (mine + t) % PER

    loads = [
        pltpu.make_async_copy(ref.at[0] if n < 3 else ref.at[0, 0], xin.at[n], in_sem.at[n])
        for n, ref in enumerate((gq, gk, gv, sq, sk, sv))
    ]
    own_rows = pl.ds(pl.multiple_of(me * TOK, TOK), TOK)
    tabs = [
        pltpu.make_async_copy(table.at[own_rows], tab.at[0], tab_sem.at[0]),
        pltpu.make_async_copy(table.at[pl.ds(0, TOK)], tab.at[1], tab_sem.at[1]),
    ]
    tabs[0].start()
    for load in loads:
        load.start()
    tabs[1].start()

    barrier = pltpu.get_barrier_semaphore()
    after = {"grp": (grp + 1) % groups, "seq": me}
    before = {"grp": (grp + groups - 1) % groups, "seq": me}

    def greet(t, _):
        pl.semaphore_signal(barrier, 1, device_id=dev((me + t) % SEQ), device_id_type=MESH)
        return 0

    lax.fori_loop(1, SEQ, greet, 0)
    pl.semaphore_signal(barrier, 1, device_id=before, device_id_type=MESH)

    turn = turn_matrix()
    low_half = lanes(TOK) < HD
    low_64 = lanes(HD) < HD

    def spread(n):
        t = tab[n]
        swapped = swap(t)
        cosine[...] = jnp.where(low_half, t, swapped)
        sine[...] = jnp.where(low_half, swapped, t)

    def rotated(x):
        turned = jnp.dot(x, turn, preferred_element_type=f32)
        return x.astype(f32) * cosine[...] + turned * sine[...]

    def cols(j):
        return pl.ds(pl.multiple_of(j * LANES, LANES), LANES)

    tabs[0].wait()
    spread(0)
    loads[0].wait()

    def pack_q(n, _):
        for u in range(4):
            j = n * 4 + u
            x = rotated(xin[0, :, cols(j)]) * (1.0 / math.sqrt(HD))
            upper, lower = x[:HD], x[HD:]
            qpack[2 * j] = jnp.where(low_64, upper, swap(lower)).astype(bf16)
            qpack[2 * j + 1] = jnp.where(low_64, swap(upper), lower).astype(bf16)
        return 0

    lax.fori_loop(0, PAIRS // 4, pack_q, 0)
    pl.semaphore_wait(barrier, SEQ)

    def q_copy(step, i, slot):
        to = target(step, i)
        return pltpu.make_async_remote_copy(
            qpack.at[to], qin.at[step, slot], q_ss.at[step, i], q_rs.at[step, slot],
            device_id=dev(to), device_id_type=MESH,
        )

    def kv_copy(step, i, slot):
        to = target(step, i)
        rows = pl.ds(pl.multiple_of(slot * TOK, TOK), TOK)
        return pltpu.make_async_remote_copy(
            kvpack.at[to], kvin.at[step, rows], kv_ss.at[step, i], kv_rs.at[step, slot],
            device_id=dev(to), device_id_type=MESH,
        )

    def o_copy(step, i):
        to = source(step, i)
        return pltpu.make_async_remote_copy(
            opack.at[step, i], o_recv.at[me], o_ss.at[step, i], o_rs.at[me],
            device_id=dev(to), device_id_type=MESH,
        )

    def send_all(copy):
        for t in range(1, PER):
            copy(0, other(t), mine).start()

        def pair(n, _):
            for i in range(PER):
                copy(2 * n + 1, i, mine).start()
                copy(2 * n + 2, i, mine).start()
            return 0

        lax.fori_loop(0, NZ // 2 - 1, pair, 0)
        for i in range(PER):
            copy(NZ - 1, i, mine).start()

    own_q = pltpu.make_async_copy(qpack.at[me], qin.at[0, mine], own_sem.at[0])
    own_kv = pltpu.make_async_copy(
        kvpack.at[me], kvin.at[0, pl.ds(pl.multiple_of(mine * TOK, TOK), TOK)], own_sem.at[1]
    )
    send_all(q_copy)
    own_q.start()

    loads[1].wait()
    loads[2].wait()

    def pack_kv(n, _):
        for u in range(4):
            j = n * 4 + u
            k = rotated(xin[1, :, cols(j)])
            v = xin[2, :, cols(j)].astype(f32)
            kvpack[2 * j] = jnp.where(low_half, k, swap(v)).astype(bf16)
            kvpack[2 * j + 1] = jnp.where(low_half, swap(k), v).astype(bf16)
        return 0

    lax.fori_loop(0, PAIRS // 4, pack_kv, 0)
    send_all(kv_copy)
    own_kv.start()

    own_len = slen[grp, me]
    own_move = smove[grp, me]
    tabs[1].wait()
    spread(1)
    for n in (3, 4, 5):
        loads[n].wait()
    slot_row = lax.broadcasted_iota(jnp.int32, (TOK, LANES), 0)
    key_live = lax.broadcasted_iota(jnp.int32, (2 * TOK, LANES), 1) < own_len
    row_live = slot_row < own_len

    def short_pair(n, _):
        for u in range(4):
            j = n * 4 + u
            q = rotated(xin[3, :, cols(j)]) * (1.0 / math.sqrt(HD))
            k = rotated(xin[4, :, cols(j)]).astype(bf16)
            stacked = jnp.concatenate([jnp.where(low_half, q, 0.0), jnp.where(low_half, 0.0, q)], 0)
            s = lax.dot_general(
                stacked.astype(bf16), k, (((1,), (1,)), ((), ())), preferred_element_type=f32
            )
            s = jnp.where(key_live, s, LOW)
            p = jnp.exp(s - jnp.max(s, axis=1, keepdims=True))
            p = jnp.where(key_live, p, 0.0).astype(bf16)
            total = jnp.dot(p, jnp.ones((TOK, LANES), bf16), preferred_element_type=f32)
            a = jnp.dot(p, xin[5, :, cols(j)], preferred_element_type=f32) / total
            result = jnp.where(row_live, jnp.where(low_half, a[:TOK], a[TOK:]), 0.0)
            stay[:, cols(j)] = jnp.where(own_move == 0, result, 0.0).astype(bf16)
            leave[:, cols(j)] = jnp.where(own_move == 1, result, 0.0).astype(bf16)
        return 0

    lax.fori_loop(0, PAIRS // 4, short_pair, 0)
    move_copy = pltpu.make_async_remote_copy(
        leave, in_out, move_sem.at[0], move_sem.at[1], device_id=after, device_id_type=MESH
    )
    move_copy.start()
    stay_copy = pltpu.make_async_copy(stay, stay_out, own_sem.at[2])
    stay_copy.start()

    acc[...] = jnp.zeros_like(acc)
    top[...] = jnp.full_like(top, LOW)
    one_lane = jnp.where(lanes(HD) == HD, 1.0, 0.0)

    def open_q(step, i):
        x = qin[step, i].astype(f32)
        rows = pl.multiple_of((step * PER + i) * TOK, TOK)
        qaug[pl.ds(rows, HD)] = jnp.where(low_64, x, one_lane).astype(bf16)
        qaug[pl.ds(rows + HD, HD)] = jnp.where(low_64, swap(x), one_lane).astype(bf16)

    def take_first(copy, own):
        own.wait()
        for t in range(1, PER):
            copy(0, other(t), other(t)).wait_recv()

    take_first(q_copy, own_q)
    for i in range(PER):
        open_q(0, i)

    def open_step(step, _):
        for i in range(PER):
            q_copy(step, i, i).wait_recv()
            open_q(step, i)
        return 0

    lax.fori_loop(1, NZ, open_step, 0)

    group_len = glen[grp]
    chunk_lane = lanes(CHUNK)
    chunk_row = lax.broadcasted_iota(jnp.int32, (CHUNK, LANES), 0)
    half_chunk = NC * TOK

    def operands(step):
        kv = kvin[step]
        zsrc = (zed + offset(step) + NZ) % NZ
        place = (
            (chunk_row // half_chunk) * (NZ * half_chunk) + zsrc * half_chunk + chunk_row % half_chunk
        )
        dead = jnp.where((chunk_lane == HD) & (place >= group_len), LOW, 0.0).astype(bf16)
        keys = jnp.where(chunk_lane < HD, kv, dead)
        values = jnp.where(chunk_lane < HD, jnp.ones((), bf16), kv)
        return keys, values

    def attend(keys, values, rows):
        s = lax.dot_general(
            qaug[rows], keys, (((1,), (1,)), ((), ())), preferred_element_type=f32
        )
        old = top[rows]
        new = jnp.maximum(old, jnp.max(s, axis=1, keepdims=True))
        p = jnp.exp(s - jnp.concatenate([new] * (CHUNK // LANES), 1))
        top[rows] = new
        acc[rows] = acc[rows] * jnp.exp(old - new) + jnp.dot(
            p.astype(bf16), values, preferred_element_type=f32
        )

    def whole_step(step):
        keys, values = operands(step)
        for half in range(2):
            attend(keys, values, pl.ds(half * HALF, HALF))

    take_first(kv_copy, own_kv)

    def one_step(step, _):
        @pl.when(step > 0)
        def _():
            for i in range(PER):
                kv_copy(step, i, i).wait_recv()

        whole_step(step)
        return 0

    lax.fori_loop(0, NZ - 1, one_step, 0)

    last = NZ - 1
    for i in range(PER):
        kv_copy(last, i, i).wait_recv()
    keys, values = operands(last)

    def close(step, i):
        rows = pl.multiple_of((step * PER + i) * TOK, TOK)
        upper, lower = acc[pl.ds(rows, HD)], acc[pl.ds(rows + HD, HD)]
        opack[step, i] = jnp.where(
            low_64, swap(upper) / upper, lower / swap(lower)
        ).astype(bf16)

    def close_step(n, high):
        step = high - n
        for i in range(PER):
            close(step, i)
            o_copy(step, i).start()
        return 0

    attend(keys, values, pl.ds(HALF, HALF))
    lax.fori_loop(0, NZ // 2, lambda n, _: close_step(n, NZ - 1), 0)
    attend(keys, values, pl.ds(0, HALF))
    lax.fori_loop(0, NZ // 2 - 1, lambda n, _: close_step(n, NZ // 2 - 1), 0)
    for t in range(1, PER):
        close(0, other(t))
        o_copy(0, other(t)).start()
    close(0, mine)
    own_o = pltpu.make_async_copy(opack.at[0, mine], o_recv.at[me], own_sem.at[3])
    own_o.start()

    for t in range(1, PER):
        q_copy(0, other(t), mine).wait_send()
        kv_copy(0, other(t), mine).wait_send()
        o_copy(0, other(t)).wait_send()

    def sent(step, _):
        for i in range(PER):
            q_copy(step, i, mine).wait_send()
            kv_copy(step, i, mine).wait_send()
            o_copy(step, i).wait_send()
        return 0

    lax.fori_loop(1, NZ, sent, 0)

    def arrived(t, _):
        head = (me + t) % SEQ
        pltpu.make_async_remote_copy(
            opack.at[0, 0], o_recv.at[head], o_ss.at[0, 0], o_rs.at[head],
            device_id=dev(head), device_id_type=MESH,
        ).wait_recv()
        return 0

    lax.fori_loop(1, SEQ, arrived, 0)
    move_copy.wait()
    stay_copy.wait()
    own_o.wait()


def unpack_kernel(glen, heads, stay, incoming, giant_out, short_out):
    me = lax.axis_index("seq")
    group_len = glen[lax.axis_index("grp")]
    low = lanes(HD) < HD
    row = me * TOK + lax.broadcasted_iota(jnp.int32, (HD, LANES), 0)
    for j in range(PAIRS):
        even, odd = heads[2 * j].astype(f32), heads[2 * j + 1].astype(f32)
        upper = jnp.where(low, even, swap(odd))
        lower = jnp.where(low, swap(even), odd)
        at = pl.ds(j * LANES, LANES)
        giant_out[0, pl.ds(0, HD), at] = jnp.where(row < group_len, upper, 0.0).astype(bf16)
        giant_out[0, pl.ds(HD, HD), at] = jnp.where(row + HD < group_len, lower, 0.0).astype(bf16)
    short_out[0, 0, 0] = stay[...]
    short_out[0, 0, 1] = incoming[...]


def per_device(table, giant_q, giant_k, giant_v, giant_len, short_q, short_k, short_v, short_len, short_move):
    any_spec = pl.BlockSpec(memory_space=pl.ANY)
    smem = pl.BlockSpec(memory_space=pltpu.SMEM)
    vmem = pl.BlockSpec(memory_space=pltpu.VMEM)
    dma = pltpu.SemaphoreType.DMA
    heads, stay, incoming = pl.pallas_call(
        main_kernel,
        out_shape=(
            jax.ShapeDtypeStruct((HEADS, HD, LANES), bf16),
            jax.ShapeDtypeStruct((TOK, FEAT), bf16),
            jax.ShapeDtypeStruct((TOK, FEAT), bf16),
        ),
        in_specs=[smem] * 3 + [any_spec] * 7,
        out_specs=(any_spec,) * 3,
        scratch_shapes=[
            pltpu.VMEM((6, TOK, FEAT), bf16),
            pltpu.VMEM((2, TOK, LANES), f32),
            pltpu.VMEM((TOK, LANES), f32),
            pltpu.VMEM((TOK, LANES), f32),
            pltpu.VMEM((SEQ, HD, LANES), bf16),
            pltpu.VMEM((SEQ, TOK, LANES), bf16),
            pltpu.VMEM((NZ, PER, HD, LANES), bf16),
            pltpu.VMEM((NZ, CHUNK, LANES), bf16),
            pltpu.VMEM((NTOK, LANES), bf16),
            pltpu.VMEM((NTOK, LANES), f32),
            pltpu.VMEM((NTOK, LANES), f32),
            pltpu.VMEM((NZ, PER, HD, LANES), bf16),
            pltpu.VMEM((TOK, FEAT), bf16),
            pltpu.VMEM((TOK, FEAT), bf16),
            dma((6,)),
            dma((2,)),
            dma((4,)),
            dma((NZ, PER)),
            dma((NZ, PER)),
            dma((NZ, PER)),
            dma((NZ, PER)),
            dma((NZ, PER)),
            dma((SEQ,)),
            dma((2,)),
        ],
        compiler_params=pltpu.CompilerParams(
            collective_id=0, has_side_effects=True, vmem_limit_bytes=56 << 20
        ),
    )(giant_len, short_len, short_move, table, giant_q, giant_k, giant_v, short_q, short_k, short_v)
    return pl.pallas_call(
        unpack_kernel,
        out_shape=(
            jax.ShapeDtypeStruct((1, TOK, FEAT), bf16),
            jax.ShapeDtypeStruct((1, 1, 2, TOK, FEAT), bf16),
        ),
        in_specs=[smem] + [vmem] * 3,
        out_specs=(vmem, vmem),
        compiler_params=pltpu.CompilerParams(vmem_limit_bytes=32 << 20),
    )(giant_len, heads, stay, incoming)


def solution(mesh):
    table = angle_table()
    in_specs = (
        P(),
        P("grp", "seq", None),
        P("grp", "seq", None),
        P("grp", "seq", None),
        P(),
        P("grp", "seq", None, None),
        P("grp", "seq", None, None),
        P("grp", "seq", None, None),
        P(),
        P(),
    )
    out_specs = (P("grp", "seq", None), P("grp", "seq", None, None, None))
    body = jax.shard_map(
        per_device, mesh=mesh, in_specs=in_specs, out_specs=out_specs, check_vma=False
    )

    def run(*arrays):
        return body(jnp.asarray(table), *arrays)

    return run
```

time: 209 us -> 83.6 us (0.40)
  Pallas kernels: 0 us -> 79.4 us
  other arithmetic: 54.2 us -> 0 us
  waiting for transfers between devices: 42.4 us -> 0 us
  matrix products: 32.3 us -> 0 us
  blocking collectives: 28.6 us -> 0 us
  starting transfers between devices: 22.4 us -> 0 us
  local copies, waits for them, and re-layouts: 25.3 us -> 3.12 us
    pallas_call x0 -> x2, Pallas kernels: none -> 79.4 us  [the longest x1 77.4 us: per_device(): pl.pallas_call(main_kernel, out_shape=(jax.ShapeDtypeStruct((HEADS, HD, L...]
    all_to_all x1 -> x0, blocking collectives: 28.6 us -> none  [per_device(): lax.all_to_all(by_heads(queries), 'seq', split_axis=1, concat_axis=0, til...]
    dot_general x17 -> x0, matrix products: 28.5 us -> none  [the longest x9 17 us: attend(): jnp.einsum('hqk,khd->qhd', weights.astype(jnp.bfloat16), value_rows, pref...]
    ppermute x1 -> x0, waiting for transfers between devices: 27.7 us -> none  [from_behind(): lax.ppermute(shard, axis, [(i, (i + by) % devices) for i in range(devices)])]
    another operation x1 -> x0, other arithmetic: 22.6 us -> none  [per_device(): attended[:, None]]
    reduce_sum x8 -> x0, other arithmetic: 20.5 us -> none  [attend(): weight_sum = jnp.sum(weights, -1)]
    all_to_all x3 -> x0, starting transfers between devices: 19.3 us -> none  [the longest x1 8.31 us: per_device(): lax.all_to_all(attended[:, None], 'seq', split_axis=0, concat_axis=1, til...]
    all_to_all x3 -> x0, waiting for transfers between devices: 14.7 us -> none  [the longest x1 14.7 us: per_device(): lax.all_to_all(by_heads(keys_rot), 'seq', split_axis=1, concat_axis=0, ti...]
  transfers between devices with their start and end apart: 4 -> 0, of which waited for: 2 -> 0; matrix products, arithmetic and copies ran while one was open for 10% -> 0% of each run, Pallas kernels for 0% -> 0%
where the time goes in v1:
time: 83.6 us; the launch traced here: 83.2 us
  Pallas kernels  79.4 us (95%)
  local copies, waits for them, and re-layouts  3.12 us (4%)
    pallas_call x1, Pallas kernels, per_device(): pl.pallas_call(main_kernel, out_shape=(jax.ShapeDtypeStruct((HEADS, HD, L...  77.4 us
    unnamed x8, local copies, waits for them, and re-layouts  3.12 us
    pallas_call x1, Pallas kernels, per_device(): pl.pallas_call(unpack_kernel, out_shape=(jax.ShapeDtypeStruct((1, TOK, FE...  1.96 us

profile of v1, /device:TPU:1, one launch (start us, length us, event | category | flops | bytes accessed | tf_op | source)
XLA Modules:
  0.0 83.2 jit_solution(3203199005149870968)
XLA Ops:
  0.6 0.0 copy-start.3
  0.6 77.4 %shard_map.113 = (bf16[32,64,128]{2,1,0:T(8,128)(2,1)}, bf16[128,2048]{1,0:T(8,128)(2,1)}, bf16[128,2048]{1,0:T(8,128)(2,1)}) custom-call(s32[16]{0:T(128)} %glen.3, s32[16,32]{1,0:T(8,128)} %slen.1, s32[16,32]{1,0:T(8,128)} %smove.1, f32[4096,128]{1,0:T(8,128)} %constant.2.clone.table, bf16[1,128,2048]{2,1,0:T(8,128)(2,1)} %gq.1, bf16[1,128,2048]{2,1,0:T(8,128)(2,1)} %gk.1, ...), custom_call_target="tpu_custom_call" | custom-call | tf_op jit(solution)/shard_map/pallas_call | solution.py:391
  78.1 0.0 copy-done.3
  78.1 0.0 copy-start
  78.1 1.0 %copy-done = bf16[32,64,128]{2,1,0:T(8,128)(2,1)S(1)} copy-done((bf16[32,64,128]{2,1,0:T(8,128)(2,1)S(1)}, bf16[32,64,128]{2,1,0:T(8,128)(2,1)}, u32[]{:S(2)}) %copy-start) | copy-done | bytes 524312
  79.1 0.0 copy-start.1
  79.1 1.0 %copy-done.1 = bf16[128,2048]{1,0:T(8,128)(2,1)S(1)} copy-done((bf16[128,2048]{1,0:T(8,128)(2,1)S(1)}, bf16[128,2048]{1,0:T(8,128)(2,1)}, u32[]{:S(2)}) %copy-start.1) | copy-done | bytes 524312
  80.1 0.0 copy-start.2
  80.1 1.0 %copy-done.2 = bf16[128,2048]{1,0:T(8,128)(2,1)S(1)} copy-done((bf16[128,2048]{1,0:T(8,128)(2,1)S(1)}, bf16[128,2048]{1,0:T(8,128)(2,1)}, u32[]{:S(2)}) %copy-start.2) | copy-done | bytes 524312
  81.2 2.0 %shard_map.114 = (bf16[1,128,2048]{2,1,0:T(8,128)(2,1)}, bf16[1,1,2,128,2048]{4,3,2,1,0:T(8,128)(2,1)}) custom-call(s32[16]{0:T(128)S(1)} %copy-done.3, bf16[32,64,128]{2,1,0:T(8,128)(2,1)S(1)} %copy-done, bf16[128,2048]{1,0:T(8,128)(2,1)S(1)} %copy-done.1, bf16[128,2048]{1,0:T(8,128)(2,1)S(1)} %copy-done.2), custom_call_target="tpu_custom_call" | custom-call | tf_op jit(solution)/shard_map/pallas_call | solution.py:430
Async XLA Ops:
  0.6 77.4 %copy-start.3 = (s32[16]{0:T(128)S(1)}, s32[16]{0:T(128)}, u32[]{:S(2)}) copy-start(s32[16]{0:T(128)} %glen.3) | copy-start | bytes 196
  78.1 1.0 %copy-start = (bf16[32,64,128]{2,1,0:T(8,128)(2,1)S(1)}, bf16[32,64,128]{2,1,0:T(8,128)(2,1)}, u32[]{:S(2)}) copy-start(bf16[32,64,128]{2,1,0:T(8,128)(2,1)} %get-tuple-element.5.heads) | copy-start | bytes 1572868
  79.1 1.0 %copy-start.1 = (bf16[128,2048]{1,0:T(8,128)(2,1)S(1)}, bf16[128,2048]{1,0:T(8,128)(2,1)}, u32[]{:S(2)}) copy-start(bf16[128,2048]{1,0:T(8,128)(2,1)} %get-tuple-element.6.stay) | copy-start | bytes 1572868
  80.1 1.0 %copy-start.2 = (bf16[128,2048]{1,0:T(8,128)(2,1)S(1)}, bf16[128,2048]{1,0:T(8,128)(2,1)}, u32[]{:S(2)}) copy-start(bf16[128,2048]{1,0:T(8,128)(2,1)} %get-tuple-element.7.incoming) | copy-start | bytes 1572868

commit v2 on v1

--- a/solution.py
+++ b/solution.py
@@ -21,6 +21,9 @@
 PER = NY * NC
 CHUNK = PER * TOK
 HALF = NTOK // 2
+HALF_BITS = (NC * TOK).bit_length() - 1
+EARLY = 4
+ROWS = 2 * CHUNK
 LOW = -1e30
 MESH = pl.DeviceIdType.MESH
 f32 = jnp.float32
@@ -58,8 +61,8 @@
 def main_kernel(
     glen, slen, smove, table, gq, gk, gv, sq, sk, sv,
     o_recv, stay_out, in_out,
-    xin, tab, cosine, sine, qpack, kvpack, qin, kvin, qaug, acc, top, opack, stay, leave,
-    in_sem, tab_sem, own_sem, q_ss, q_rs, kv_ss, kv_rs, o_ss, o_rs, move_sem,
+    xin, tab, cosine, sine, qpack, kvpack, qin, kvin, qaug, acc, top, late_k, late_v, opack, stay, leave,
+    in_sem, tab_sem, own_sem, q_ss, q_rs, kv_ss, kv_rs, o_ss, o_rs, move_ss, move_rs,
 ):
     me = lax.axis_index("seq")
     grp = lax.axis_index("grp")
@@ -128,16 +131,6 @@
     spread(0)
     loads[0].wait()
 
-    def pack_q(n, _):
-        for u in range(4):
-            j = n * 4 + u
-            x = rotated(xin[0, :, cols(j)]) * (1.0 / math.sqrt(HD))
-            upper, lower = x[:HD], x[HD:]
-            qpack[2 * j] = jnp.where(low_64, upper, swap(lower)).astype(bf16)
-            qpack[2 * j + 1] = jnp.where(low_64, swap(upper), lower).astype(bf16)
-        return 0
-
-    lax.fori_loop(0, PAIRS // 4, pack_q, 0)
     pl.semaphore_wait(barrier, SEQ)
 
     def q_copy(step, i, slot):
@@ -162,26 +155,33 @@
             device_id=dev(to), device_id_type=MESH,
         )
 
-    def send_all(copy):
+    def pack_q(step, y):
+        j = y * NZ + (zed - offset(step) + NZ) % NZ
+        x = rotated(xin[0, :, cols(j)]) * (1.0 / math.sqrt(HD))
+        upper, lower = x[:HD], x[HD:]
+        qpack[2 * j] = jnp.where(low_64, upper, swap(lower)).astype(bf16)
+        qpack[2 * j + 1] = jnp.where(low_64, swap(upper), lower).astype(bf16)
+
+    def send_q(step, _):
+        for y in range(NY):
+            pack_q(step, y)
+            for c in range(NC):
+                q_copy(step, y * NC + c, mine).start()
+        return 0
+
+    def send_first(copy):
         for t in range(1, PER):
             copy(0, other(t), mine).start()
-
-        def pair(n, _):
-            for i in range(PER):
-                copy(2 * n + 1, i, mine).start()
-                copy(2 * n + 2, i, mine).start()
-            return 0
-
-        lax.fori_loop(0, NZ // 2 - 1, pair, 0)
-        for i in range(PER):
-            copy(NZ - 1, i, mine).start()
 
     own_q = pltpu.make_async_copy(qpack.at[me], qin.at[0, mine], own_sem.at[0])
     own_kv = pltpu.make_async_copy(
         kvpack.at[me], kvin.at[0, pl.ds(pl.multiple_of(mine * TOK, TOK), TOK)], own_sem.at[1]
     )
-    send_all(q_copy)
+    for y in range(NY):
+        pack_q(0, y)
+    send_first(q_copy)
     own_q.start()
+    lax.fori_loop(1, NZ, send_q, 0)
 
     loads[1].wait()
     loads[2].wait()
@@ -196,9 +196,6 @@
         return 0
 
     lax.fori_loop(0, PAIRS // 4, pack_kv, 0)
-    send_all(kv_copy)
-    own_kv.start()
-
     own_len = slen[grp, me]
     own_move = smove[grp, me]
     tabs[1].wait()
@@ -229,10 +226,27 @@
         return 0
 
     lax.fori_loop(0, PAIRS // 4, short_pair, 0)
-    move_copy = pltpu.make_async_remote_copy(
-        leave, in_out, move_sem.at[0], move_sem.at[1], device_id=after, device_id_type=MESH
-    )
-    move_copy.start()
+    send_first(kv_copy)
+    own_kv.start()
+
+    def send_pair(n, _):
+        for i in range(PER):
+            kv_copy(2 * n + 1, i, mine).start()
+            kv_copy(2 * n + 2, i, mine).start()
+        return 0
+
+    lax.fori_loop(0, NZ // 2 - 1, send_pair, 0)
+    for i in range(PER):
+        kv_copy(NZ - 1, i, mine).start()
+
+
+    def move_copy(n):
+        rows = pl.ds(pl.multiple_of(n * (TOK // NZ), TOK // NZ), TOK // NZ)
+        return pltpu.make_async_remote_copy(
+            leave.at[rows], in_out.at[rows], move_ss.at[n], move_rs.at[n],
+            device_id=after, device_id_type=MESH,
+        )
+
     stay_copy = pltpu.make_async_copy(stay, stay_out, own_sem.at[2])
     stay_copy.start()
 
@@ -251,16 +265,15 @@
         for t in range(1, PER):
             copy(0, other(t), other(t)).wait_recv()
 
-    take_first(q_copy, own_q)
-    for i in range(PER):
-        open_q(0, i)
-
     def open_step(step, _):
         for i in range(PER):
             q_copy(step, i, i).wait_recv()
             open_q(step, i)
         return 0
 
+    take_first(q_copy, own_q)
+    for i in range(PER):
+        open_q(0, i)
     lax.fori_loop(1, NZ, open_step, 0)
 
     group_len = glen[grp]
@@ -272,7 +285,9 @@
         kv = kvin[step]
         zsrc = (zed + offset(step) + NZ) % NZ
         place = (
-            (chunk_row // half_chunk) * (NZ * half_chunk) + zsrc * half_chunk + chunk_row % half_chunk
+            (chunk_row >> HALF_BITS) * (NZ * half_chunk)
+            + zsrc * half_chunk
+            + (chunk_row & (half_chunk - 1))
         )
         dead = jnp.where((chunk_lane == HD) & (place >= group_len), LOW, 0.0).astype(bf16)
         keys = jnp.where(chunk_lane < HD, kv, dead)
@@ -285,16 +300,11 @@
         )
         old = top[rows]
         new = jnp.maximum(old, jnp.max(s, axis=1, keepdims=True))
-        p = jnp.exp(s - jnp.concatenate([new] * (CHUNK // LANES), 1))
+        p = jnp.exp(s - jnp.concatenate([new] * (keys.shape[0] // LANES), 1))
         top[rows] = new
         acc[rows] = acc[rows] * jnp.exp(old - new) + jnp.dot(
             p.astype(bf16), values, preferred_element_type=f32
         )
-
-    def whole_step(step):
-        keys, values = operands(step)
-        for half in range(2):
-            attend(keys, values, pl.ds(half * HALF, HALF))
 
     take_first(kv_copy, own_kv)
 
@@ -304,15 +314,30 @@
             for i in range(PER):
                 kv_copy(step, i, i).wait_recv()
 
-        whole_step(step)
-        return 0
-
-    lax.fori_loop(0, NZ - 1, one_step, 0)
-
-    last = NZ - 1
-    for i in range(PER):
-        kv_copy(last, i, i).wait_recv()
-    keys, values = operands(last)
+        keys, values = operands(step)
+        attend(keys, values, pl.ds(0, HALF))
+
+        move_copy(2 * step).start()
+        attend(keys, values, pl.ds(HALF, HALF))
+        move_copy(2 * step + 1).start()
+        return 0
+
+    lax.fori_loop(0, EARLY, one_step, 0)
+
+    def ready(step, _):
+        for i in range(PER):
+            kv_copy(step, i, i).wait_recv()
+        rows = pl.ds(pl.multiple_of((step - EARLY) * CHUNK, CHUNK), CHUNK)
+        late_k[rows], late_v[rows] = operands(step)
+        return 0
+
+    lax.fori_loop(EARLY, NZ, ready, 0)
+
+    def rest(group):
+        rows = pl.ds(pl.multiple_of(group * ROWS, ROWS), ROWS)
+        for n in range((NZ - EARLY) // 2):
+            at = pl.ds(n * 2 * CHUNK, 2 * CHUNK)
+            attend(late_k[at], late_v[at], rows)
 
     def close(step, i):
         rows = pl.multiple_of((step * PER + i) * TOK, TOK)
@@ -321,17 +346,20 @@
             low_64, swap(upper) / upper, lower / swap(lower)
         ).astype(bf16)
 
-    def close_step(n, high):
-        step = high - n
-        for i in range(PER):
-            close(step, i)
-            o_copy(step, i).start()
-        return 0
-
-    attend(keys, values, pl.ds(HALF, HALF))
-    lax.fori_loop(0, NZ // 2, lambda n, _: close_step(n, NZ - 1), 0)
-    attend(keys, values, pl.ds(0, HALF))
-    lax.fori_loop(0, NZ // 2 - 1, lambda n, _: close_step(n, NZ // 2 - 1), 0)
+    def finish(n, _):
+        group = NZ // 2 - 1 - n
+        rest(group)
+        for step in (2 * group + 1, 2 * group):
+            for i in range(PER):
+                close(step, i)
+                o_copy(step, i).start()
+        return 0
+
+    lax.fori_loop(0, NZ // 2 - 1, finish, 0)
+    rest(0)
+    for i in range(PER):
+        close(1, i)
+        o_copy(1, i).start()
     for t in range(1, PER):
         close(0, other(t))
         o_copy(0, other(t)).start()
@@ -362,31 +390,68 @@
         return 0
 
     lax.fori_loop(1, SEQ, arrived, 0)
-    move_copy.wait()
+
+    def moved(n, _):
+        move_copy(n).wait()
+        return 0
+
+    lax.fori_loop(0, NZ, moved, 0)
     stay_copy.wait()
     own_o.wait()
 
 
-def unpack_kernel(glen, heads, stay, incoming, giant_out, short_out):
+PARTS = 4
+
+
+def unpack_kernel(glen, heads, stay, incoming, giant_out, short_out, held, made, both, sems):
+    moves = [
+        pltpu.make_async_copy(ref, both.at[n], sems.at[n]) for n, ref in enumerate((stay, incoming))
+    ]
+    ends = [
+        pltpu.make_async_copy(both.at[n], short_out.at[0, 0, n], sems.at[2 + 2 * PARTS + n])
+        for n in range(2)
+    ]
+    per = HEADS // PARTS
+    wide = FEAT // PARTS
+    into = [
+        pltpu.make_async_copy(
+            heads.at[pl.ds(n * per, per)], held.at[pl.ds(n * per, per)], sems.at[2 + n]
+        )
+        for n in range(PARTS)
+    ]
+    out = [
+        pltpu.make_async_copy(
+            made.at[:, pl.ds(n * wide, wide)], giant_out.at[0, :, pl.ds(n * wide, wide)],
+            sems.at[2 + PARTS + n],
+        )
+        for n in range(PARTS)
+    ]
+    for copy in moves + into:
+        copy.start()
+    for copy, end in zip(moves, ends):
+        copy.wait()
+        end.start()
     me = lax.axis_index("seq")
     group_len = glen[lax.axis_index("grp")]
     low = lanes(HD) < HD
     row = me * TOK + lax.broadcasted_iota(jnp.int32, (HD, LANES), 0)
-    for j in range(PAIRS):
-        even, odd = heads[2 * j].astype(f32), heads[2 * j + 1].astype(f32)
-        upper = jnp.where(low, even, swap(odd))
-        lower = jnp.where(low, swap(even), odd)
-        at = pl.ds(j * LANES, LANES)
-        giant_out[0, pl.ds(0, HD), at] = jnp.where(row < group_len, upper, 0.0).astype(bf16)
-        giant_out[0, pl.ds(HD, HD), at] = jnp.where(row + HD < group_len, lower, 0.0).astype(bf16)
-    short_out[0, 0, 0] = stay[...]
-    short_out[0, 0, 1] = incoming[...]
+    for n in range(PARTS):
+        into[n].wait()
+        for j in range(n * PAIRS // PARTS, (n + 1) * PAIRS // PARTS):
+            even, odd = held[2 * j].astype(f32), held[2 * j + 1].astype(f32)
+            upper = jnp.where(low, even, swap(odd))
+            lower = jnp.where(low, swap(even), odd)
+            at = pl.ds(j * LANES, LANES)
+            made[pl.ds(0, HD), at] = jnp.where(row < group_len, upper, 0.0).astype(bf16)
+            made[pl.ds(HD, HD), at] = jnp.where(row + HD < group_len, lower, 0.0).astype(bf16)
+        out[n].start()
+    for copy in out + ends:
+        copy.wait()
 
 
 def per_device(table, giant_q, giant_k, giant_v, giant_len, short_q, short_k, short_v, short_len, short_move):
     any_spec = pl.BlockSpec(memory_space=pl.ANY)
     smem = pl.BlockSpec(memory_space=pltpu.SMEM)
-    vmem = pl.BlockSpec(memory_space=pltpu.VMEM)
     dma = pltpu.SemaphoreType.DMA
     heads, stay, incoming = pl.pallas_call(
         main_kernel,
@@ -409,6 +474,8 @@
             pltpu.VMEM((NTOK, LANES), bf16),
             pltpu.VMEM((NTOK, LANES), f32),
             pltpu.VMEM((NTOK, LANES), f32),
+            pltpu.VMEM(((NZ - EARLY) * CHUNK, LANES), bf16),
+            pltpu.VMEM(((NZ - EARLY) * CHUNK, LANES), bf16),
             pltpu.VMEM((NZ, PER, HD, LANES), bf16),
             pltpu.VMEM((TOK, FEAT), bf16),
             pltpu.VMEM((TOK, FEAT), bf16),
@@ -421,7 +488,8 @@
             dma((NZ, PER)),
             dma((NZ, PER)),
             dma((SEQ,)),
-            dma((2,)),
+            dma((NZ,)),
+            dma((NZ,)),
         ],
         compiler_params=pltpu.CompilerParams(
             collective_id=0, has_side_effects=True, vmem_limit_bytes=56 << 20
@@ -433,9 +501,15 @@
             jax.ShapeDtypeStruct((1, TOK, FEAT), bf16),
             jax.ShapeDtypeStruct((1, 1, 2, TOK, FEAT), bf16),
         ),
-        in_specs=[smem] + [vmem] * 3,
-        out_specs=(vmem, vmem),
-        compiler_params=pltpu.CompilerParams(vmem_limit_bytes=32 << 20),
+        in_specs=[smem] + [any_spec] * 3,
+        out_specs=(any_spec, any_spec),
+        scratch_shapes=[
+            pltpu.VMEM((HEADS, HD, LANES), bf16),
+            pltpu.VMEM((TOK, FEAT), bf16),
+            pltpu.VMEM((2, TOK, FEAT), bf16),
+            dma((4 + 2 * PARTS,)),
+        ],
+        compiler_params=pltpu.CompilerParams(vmem_limit_bytes=56 << 20),
     )(giant_len, heads, stay, incoming)
 
 

time: 83.6 us -> 76.1 us (0.910); the launches traced: 83.2 us -> 74.8 us
  Pallas kernels: 79.4 us -> 74.2 us
  local copies, waits for them, and re-layouts: 3.12 us -> 0 us
    pallas_call x1, Pallas kernels: 77.4 us -> 71.1 us  [per_device(): pl.pallas_call(main_kernel, out_shape=(jax.ShapeDtypeStruct((HEADS, HD, L...]
    unnamed x8 -> x0, local copies, waits for them, and re-layouts: 3.12 us -> none
    pallas_call x1, Pallas kernels: 1.96 us -> 3.1 us  [per_device(): pl.pallas_call(unpack_kernel, out_shape=(jax.ShapeDtypeStruct((1, TOK, FE...]
where the time goes in v2:
time: 76.1 us; the launch traced here: 74.8 us
  Pallas kernels  74.2 us (98%)
    pallas_call x1, Pallas kernels, per_device(): pl.pallas_call(main_kernel, out_shape=(jax.ShapeDtypeStruct((HEADS, HD, L...  71.1 us
    pallas_call x1, Pallas kernels, per_device(): pl.pallas_call(unpack_kernel, out_shape=(jax.ShapeDtypeStruct((1, TOK, FE...  3.1 us

profile of v2, /device:TPU:1, one launch (start us, length us, event | category | flops | bytes accessed | tf_op | source)
XLA Modules:
  0.0 74.8 jit_solution(3074932664440961884)
XLA Ops:
  0.6 71.1 %shard_map.113 = (bf16[32,64,128]{2,1,0:T(8,128)(2,1)}, bf16[128,2048]{1,0:T(8,128)(2,1)}, bf16[128,2048]{1,0:T(8,128)(2,1)}) custom-call(s32[16]{0:T(128)} %glen.3, s32[16,32]{1,0:T(8,128)} %slen.1, s32[16,32]{1,0:T(8,128)} %smove.1, f32[4096,128]{1,0:T(8,128)} %constant.2.clone.table, bf16[1,128,2048]{2,1,0:T(8,128)(2,1)} %gq.1, bf16[1,128,2048]{2,1,0:T(8,128)(2,1)} %gk.1, ...), custom_call_target="tpu_custom_call" | custom-call | tf_op jit(solution)/shard_map/pallas_call | solution.py:456
  71.7 3.1 %shard_map.114 = (bf16[1,128,2048]{2,1,0:T(8,128)(2,1)}, bf16[1,1,2,128,2048]{4,3,2,1,0:T(8,128)(2,1)}) custom-call(s32[16]{0:T(128)} %glen.3, bf16[32,64,128]{2,1,0:T(8,128)(2,1)} %get-tuple-element.5.heads, bf16[128,2048]{1,0:T(8,128)(2,1)} %get-tuple-element.6.stay, bf16[128,2048]{1,0:T(8,128)(2,1)} %get-tuple-element.7.incoming), custom_call_target="tpu_custom_call" | custom-call | tf_op jit(solution)/shard_map/pallas_call | solution.py:498

commit v3 on v2

--- a/solution.py
+++ b/solution.py
@@ -22,7 +22,7 @@
 CHUNK = PER * TOK
 HALF = NTOK // 2
 HALF_BITS = (NC * TOK).bit_length() - 1
-EARLY = 4
+EARLY = 6
 ROWS = 2 * CHUNK
 LOW = -1e30
 MESH = pl.DeviceIdType.MESH
@@ -317,14 +317,14 @@
         keys, values = operands(step)
         attend(keys, values, pl.ds(0, HALF))
 
-        move_copy(2 * step).start()
+        move_copy(step).start()
         attend(keys, values, pl.ds(HALF, HALF))
-        move_copy(2 * step + 1).start()
         return 0
 
     lax.fori_loop(0, EARLY, one_step, 0)
 
     def ready(step, _):
+        move_copy(step).start()
         for i in range(PER):
             kv_copy(step, i, i).wait_recv()
         rows = pl.ds(pl.multiple_of((step - EARLY) * CHUNK, CHUNK), CHUNK)
@@ -426,11 +426,8 @@
         )
         for n in range(PARTS)
     ]
-    for copy in moves + into:
+    for copy in into[:1] + moves + into[1:]:
         copy.start()
-    for copy, end in zip(moves, ends):
-        copy.wait()
-        end.start()
     me = lax.axis_index("seq")
     group_len = glen[lax.axis_index("grp")]
     low = lanes(HD) < HD
@@ -445,6 +442,9 @@
             made[pl.ds(0, HD), at] = jnp.where(row < group_len, upper, 0.0).astype(bf16)
             made[pl.ds(HD, HD), at] = jnp.where(row + HD < group_len, lower, 0.0).astype(bf16)
         out[n].start()
+        if n < 2:
+            moves[n].wait()
+            ends[n].start()
     for copy in out + ends:
         copy.wait()
 

time: 76.1 us -> 74.3 us (0.976)
  Pallas kernels: 74.2 us -> 73 us
    pallas_call x1, Pallas kernels: 71.1 us -> 69.9 us  [per_device(): pl.pallas_call(main_kernel, out_shape=(jax.ShapeDtypeStruct((HEADS, HD, L...]
where the time goes in v3:
time: 74.3 us; the launch traced here: 73.6 us
  Pallas kernels  73 us (98%)
    pallas_call x1, Pallas kernels, per_device(): pl.pallas_call(main_kernel, out_shape=(jax.ShapeDtypeStruct((HEADS, HD, L...  69.9 us
    pallas_call x1, Pallas kernels, per_device(): pl.pallas_call(unpack_kernel, out_shape=(jax.ShapeDtypeStruct((1, TOK, FE...  3.09 us

profile of v3, /device:TPU:1, one launch (start us, length us, event | category | flops | bytes accessed | tf_op | source)
XLA Modules:
  0.0 73.6 jit_solution(10379944533976884401)
XLA Ops:
  0.6 69.9 %shard_map.113 = (bf16[32,64,128]{2,1,0:T(8,128)(2,1)}, bf16[128,2048]{1,0:T(8,128)(2,1)}, bf16[128,2048]{1,0:T(8,128)(2,1)}) custom-call(s32[16]{0:T(128)} %glen.3, s32[16,32]{1,0:T(8,128)} %slen.1, s32[16,32]{1,0:T(8,128)} %smove.1, f32[4096,128]{1,0:T(8,128)} %constant.2.clone.table, bf16[1,128,2048]{2,1,0:T(8,128)(2,1)} %gq.1, bf16[1,128,2048]{2,1,0:T(8,128)(2,1)} %gk.1, ...), custom_call_target="tpu_custom_call" | custom-call | tf_op jit(solution)/shard_map/pallas_call | solution.py:456
  70.6 3.1 %shard_map.114 = (bf16[1,128,2048]{2,1,0:T(8,128)(2,1)}, bf16[1,1,2,128,2048]{4,3,2,1,0:T(8,128)(2,1)}) custom-call(s32[16]{0:T(128)} %glen.3, bf16[32,64,128]{2,1,0:T(8,128)(2,1)} %get-tuple-element.5.heads, bf16[128,2048]{1,0:T(8,128)(2,1)} %get-tuple-element.6.stay, bf16[128,2048]{1,0:T(8,128)(2,1)} %get-tuple-element.7.incoming), custom_call_target="tpu_custom_call" | custom-call | tf_op jit(solution)/shard_map/pallas_call | solution.py:498
